TPU v7x, 32 devices: a whole 2x2x4 slice. The times are simulated.
32 devices in a mesh: seq: 8 (over y, x, core), exp: 4 (over z).
Axes of the slice: x: 2, y: 2, z: 4, core: 2. Of those that a mesh axis runs over, the one named last changes fastest.
Arguments:
- hidden: bfloat16 [1024, 4096], P('seq', 'exp'), may hold values from -6 to 6
- queries: bfloat16 [1024, 4096], P('seq', 'exp'), may hold values from -40 to 40
- keys: bfloat16 [1024, 1024], P('seq', 'exp'), may hold values from -6 to 6
- values: bfloat16 [1024, 1024], P('seq', 'exp'), may hold values from -6 to 6
- block_place: int32 [16], replicated, may hold values from 0 to 15, as said below
- page_table: int32 [64], replicated, may hold values from 0 to 63, each once
- out_weight: bfloat16 [4096, 4096], P('exp'), may hold values from -0.09375 to 0.09375
- norm_gain: float32 [4096], replicated, may hold values from 0.5 to 2
- gate_probs: float32 [1024, 2], P('seq'), may hold values from 0.1 to 1
- routes: int32 [1024, 2], P('seq'), may hold values from 0 to 7, all different within a row; in each aligned block of 128 rows (0 to 127, 128 to 255, ...) at most 64 rows name the same one
- w_gate: bfloat16 [8, 4096, 14336], P('exp', None, 'seq'), may hold values from -0.09375 to 0.09375
- w_up: bfloat16 [8, 4096, 14336], P('exp', None, 'seq'), may hold values from -0.09375 to 0.09375
- w_down: bfloat16 [8, 14336, 4096], P('exp', 'seq'), may hold values from -0.046875 to 0.046875
Outputs:
- layer_out: bfloat16 [1024, 4096], P('seq', 'exp')
- key_value_pages: bfloat16 [64, 16, 2, 1024], P('seq', None, None, 'exp')
Inputs may be any that keep to these rules, and one draw needn't show every extreme that they name: `block_place`: the first 12 entries are a permutation of 0 to 11, the others a permutation of 12 to 15. `page_table`: A permutation of the pages. `routes`: in the rows of one index of seq (128 rows) no expert is named more than 64 times, a bound that some block reaches; a row names two different experts.
All inputs are finite; a program needn't handle non-finite values.
Results may differ from a plain program's by a relative error of at most 0.02.
Values may be sent and summed in bfloat16 or wider, within the bound.
A program may use at most 192 MiB of HBM per device.

v0:
```python
import math

import jax
import jax.numpy as jnp
from jax import lax
from jax.sharding import PartitionSpec as P

HEAD_SIZE = 128
NEXP = 8
PAGE_TOKENS = 16


THETA = 1000000.0
EPS = 1e-05


def apply_rotary(values_in, positions, head_count):
    row_count = values_in.shape[0]
    split_view = values_in.astype(jnp.float32).reshape(row_count, head_count, HEAD_SIZE)
    steps_half = jnp.arange(HEAD_SIZE // 2, dtype=jnp.float32)
    frequency = THETA ** (-(2.0 * steps_half) / HEAD_SIZE)
    angles = positions.astype(jnp.float32)[:, None] * frequency[None, :]
    cosine = jnp.cos(angles)[:, None, :]
    sine_part = jnp.sin(angles)[:, None, :]
    front_half = split_view[..., : HEAD_SIZE // 2]
    back_half = split_view[..., HEAD_SIZE // 2 :]
    turned = jnp.concatenate(
        [front_half * cosine - back_half * sine_part, back_half * cosine + front_half * sine_part],
        axis=-1,
    )
    return turned.reshape(row_count, head_count * HEAD_SIZE).astype(jnp.bfloat16)


def per_device(
    hidden,
    queries,
    keys,
    values,
    block_place,
    page_table,
    out_weight,
    norm_gain,
    gate_probs,
    routes,
    w_gate,
    w_up,
    w_down,
):
    seq_count = lax.axis_size("seq")
    exp_count = lax.axis_size("exp")
    seq_index = lax.axis_index("seq")
    tok_rows = queries.shape[0]
    half_rows = tok_rows // 2
    all_rows = tok_rows * seq_count
    long_len = 3 * all_rows // 4
    every_row = jnp.arange(all_rows, dtype=jnp.int32)
    all_pos = block_place[every_row // half_rows] * half_rows + every_row % half_rows
    my_pos = lax.dynamic_slice_in_dim(all_pos, seq_index * tok_rows, tok_rows)
    my_long = my_pos >= long_len
    my_rope = my_pos - long_len * my_long.astype(jnp.int32)
    q_heads = queries.shape[1] // HEAD_SIZE
    kv_heads = keys.shape[1] // HEAD_SIZE
    query_head_group = q_heads // kv_heads
    query_rotated = apply_rotary(queries, my_rope, q_heads)
    key_rotated = apply_rotary(keys, my_rope, kv_heads)
    q_grid = query_rotated.reshape(tok_rows, kv_heads, query_head_group, HEAD_SIZE)
    score_scale = 1.0 / math.sqrt(HEAD_SIZE)
    page_count = tok_rows // PAGE_TOKENS
    inverse_table = jnp.argsort(page_table)
    my_logical = lax.dynamic_slice_in_dim(inverse_table, seq_index * page_count, page_count)
    row_at = jnp.argsort(all_pos)
    taken = row_at[
        (
            my_logical[:, None] * PAGE_TOKENS + jnp.arange(PAGE_TOKENS, dtype=jnp.int32)[None, :]
        ).reshape(page_count * PAGE_TOKENS)
    ]
    key_all, value_all = (
        lax.all_gather(key_rotated, "seq", axis=0, tiled=True),
        lax.all_gather(values, "seq", axis=0, tiled=True),
    )
    peak_old = jnp.full((kv_heads, query_head_group, tok_rows), -1e30, jnp.float32)
    row_count = key_all.shape[0]
    scores = (
        jnp.einsum(
            "tkgd,nkd->kgtn",
            q_grid,
            key_all.reshape(row_count, kv_heads, HEAD_SIZE),
            preferred_element_type=jnp.float32,
        )
        * score_scale
    )
    allowed = ((all_pos >= long_len)[None, :] == my_long[:, None]) & (
        all_pos[None, :] <= my_pos[:, None]
    )
    scores = jnp.where(allowed, scores, -1e30)
    peak_new = jnp.maximum(peak_old, jnp.max(scores, axis=-1))
    weights = jnp.where(allowed, jnp.exp(scores - peak_new[..., None]), 0.0)
    total_new = jnp.sum(weights, axis=-1)
    summed = jnp.einsum(
        "kgtn,nkd->kgtd",
        weights.astype(jnp.bfloat16),
        value_all.reshape(row_count, kv_heads, HEAD_SIZE),
        preferred_element_type=jnp.float32,
    )
    peak_final, total_final, summed = (peak_new, total_new, summed)
    cache_pages = jnp.stack([key_all[taken], value_all[taken]], axis=1).reshape(
        page_count, PAGE_TOKENS, 2, kv_heads * HEAD_SIZE
    )
    attended = (
        (summed / total_final[..., None])
        .transpose(2, 0, 1, 3)
        .reshape(tok_rows, q_heads * HEAD_SIZE)
        .astype(jnp.bfloat16)
    )
    partial_proj = jnp.dot(attended, out_weight, preferred_element_type=jnp.float32)
    projected = lax.psum_scatter(
        partial_proj.astype(jnp.bfloat16), "exp", scatter_dimension=1, tiled=True
    ).astype(jnp.float32)
    residual = (hidden.astype(jnp.float32) + projected).astype(jnp.bfloat16)
    top_count = routes.shape[1]
    capacity = tok_rows // 2
    assign_count = tok_rows * top_count
    flat_routes = routes.reshape(assign_count)
    expert_hot = (flat_routes[:, None] == jnp.arange(NEXP, dtype=jnp.int32)[None, :]).astype(
        jnp.float32
    )
    earlier = (jnp.arange(assign_count)[:, None] > jnp.arange(assign_count)[None, :]).astype(
        jnp.float32
    )
    before = jnp.dot(earlier, expert_hot, preferred_element_type=jnp.float32)
    slot_rank = jnp.sum(before * expert_hot, axis=1).astype(jnp.int32).reshape(tok_rows, top_count)
    slot_grid = routes * capacity + slot_rank
    chooser = jnp.any(
        slot_grid[None, :, :] == jnp.arange(NEXP * capacity, dtype=jnp.int32)[:, None, None],
        axis=-1,
    ).astype(jnp.bfloat16)
    outgoing_rows = jnp.dot(chooser, residual, preferred_element_type=jnp.float32).astype(
        jnp.bfloat16
    )
    expert_local = NEXP // exp_count
    arrived_rows = lax.all_to_all(
        outgoing_rows.reshape(exp_count, expert_local * capacity, -1),
        "exp",
        split_axis=0,
        concat_axis=2,
        tiled=True,
    )
    gathered_in = arrived_rows.reshape(expert_local, capacity, -1).astype(jnp.float32)
    mean_square = jnp.mean(gathered_in * gathered_in, axis=-1, keepdims=True)
    normed = (gathered_in * lax.rsqrt(mean_square + EPS) * norm_gain).astype(jnp.bfloat16)
    token_rows = lax.all_gather(normed, "seq", axis=1, tiled=True)
    gate_part = jnp.einsum("end,edf->enf", token_rows, w_gate, preferred_element_type=jnp.float32)
    up_part = jnp.einsum("end,edf->enf", token_rows, w_up, preferred_element_type=jnp.float32)
    hidden_units = (jax.nn.silu(gate_part) * up_part).astype(jnp.bfloat16)
    returned = lax.psum_scatter(
        jnp.einsum("enf,efd->ned", hidden_units, w_down, preferred_element_type=jnp.float32).astype(
            jnp.bfloat16
        ),
        "seq",
        scatter_dimension=0,
        tiled=True,
    )
    homed = lax.all_to_all(returned, "exp", split_axis=2, concat_axis=1, tiled=True)
    lookup = homed.reshape(capacity * NEXP, -1)
    chosen = (
        lookup[(slot_rank * NEXP + routes).reshape(assign_count)]
        .astype(jnp.float32)
        .reshape(tok_rows, top_count, -1)
    )
    gate_share = gate_probs / jnp.sum(gate_probs, axis=1, keepdims=True)
    layer_out = (
        residual.astype(jnp.float32) + jnp.sum(gate_share[:, :, None] * chosen, axis=1)
    ).astype(jnp.bfloat16)
    return (layer_out, cache_pages)


def solution(mesh):
    return jax.shard_map(
        per_device,
        mesh=mesh,
        in_specs=(
            P("seq", "exp"),
            P("seq", "exp"),
            P("seq", "exp"),
            P("seq", "exp"),
            P(),
            P(),
            P("exp", None),
            P(),
            P("seq", None),
            P("seq", None),
            P("exp", None, "seq"),
            P("exp", None, "seq"),
            P("exp", "seq", None),
        ),
        out_specs=(P("seq", "exp"), P("seq", None, None, "exp")),
        check_vma=False,
    )
```

profile of v0, /device:TPU:0, one launch (start us, length us, event | category | flops | bytes accessed | tf_op | source)
XLA Modules:
  0.0 367.2 jit_solution(10163866305850828647)
XLA Ops:
  7.6 1.9 fusion.30
  9.5 4.4 %compare_select_fusion.1 = s32[1024,1]{0,1:T(1,128)S(1)} fusion(s32[]{:T(128)} %bitcast.9, s32[]{:T(128)} %bitcast.10, s32[]{:T(128)} %bitcast.11, s32[]{:T(128)} %bitcast.12, s32[]{:T(128)} %bitcast.13, s32[]{:T(128)} %bitcast.15, s32[]{:T(128)} %bitcast.14), kind=kLoop, calls=%fused_computation.53 | loop fusion | flops 23552 | bytes 4124 | tf_op jit(solution)/shard_map/gather | solution.py:57
  13.9 5.7 %broadcast_compare_fusion = (pred[1024]{0:T(1024)(128)(4,1)S(1)}, s32[1024]{0:T(1024)S(1)}) fusion(pred[1024]{0:T(1024)(128)(4,1)S(1)} %compare_reduce_fusion, pred[1024]{0:T(1024)(128)(4,1)S(1)} %compare_reduce_fusion.1, pred[1024]{0:T(1024)(128)(4,1)S(1)} %compare_reduce_fusion.2, pred[1024]{0:T(1024)(128)(4,1)S(1)} %compare_reduce_fusion.3, ...), kind=kLoop, calls=%fused_computation.80 | loop fusion | flops 18432 | bytes 18468 | tf_op jit(solution)/shard_map/ge | solution.py:92
  21.4 11.3 %all_gather.9 = bf16[1024,256]{1,0:T(8,128)(2,1)S(1)} all-gather(bf16[128,256]{1,0:T(8,128)(2,1)S(1)} %bitcast.104), channel_id=1, replica_groups=mesh['seq'=8,'exp'=4] {'seq'}, dimensions={0}, use_global_device_ids=true | all-gather | bytes 589824 | tf_op jit(solution)/shard_map/all_gather | solution.py:78
  32.9 9.8 %all_gather.10 = bf16[1024,256]{1,0:T(8,128)(2,1)S(1)} all-gather(bf16[128,256]{1,0:T(8,128)(2,1)} %param.16), channel_id=1, replica_groups=mesh['seq'=8,'exp'=4] {'seq'}, dimensions={0}, use_global_device_ids=true | all-gather | bytes 589824 | tf_op jit(solution)/shard_map/all_gather | solution.py:79
  44.9 1.0 fusion.1
  46.0 1.2 fusion.14
  47.2 1.1 slice-done.1
  48.2 2.3 convolution_convert_fusion
  51.3 26.8 %reduce-scatter.3.cloned.1.call-done = bf16[128,1024]{1,0:T(8,128)(2,1)} async-done(((bf16[128,4096]{1,0:T(8,128)(2,1)}), bf16[128,1024]{1,0:T(8,128)(2,1)}) %reduce-scatter.3.cloned.1.call-update) | async-done | bytes 262160 | tf_op jit(solution)/shard_map/reduce_scatter | solution.py:116
  78.1 1.4 convolution_convert_fusion.1
  79.5 28.2 %all_to_all.24 = bf16[4,128,1024]{2,1,0:T(8,128)(2,1)S(1)} all-to-all(bf16[4,128,1024]{2,1,0:T(8,128)(2,1)S(1)} %bitcast.98), channel_id=1, replica_groups=mesh['seq'=8,'exp'=4] {'exp'}, dimensions={0} | all-to-all | bytes 2097152 | tf_op jit(solution)/shard_map/all_to_all | solution.py:141
  108.4 2.7 copy.82
  111.1 2.7 reshape.287
  113.8 2.1 multiply_convert_fusion.1
  116.0 53.6 %all-gather.2.cloned.1.call-done = bf16[2,512,4096]{2,1,0:T(8,128)(2,1)} async-done(((bf16[2,64,4096]{2,1,0:T(8,128)(2,1)}), bf16[2,512,4096]{2,1,0:T(8,128)(2,1)}) %all-gather.2.cloned.1.call-update) | async-done | bytes 8388624 | tf_op jit(solution)/shard_map/all_gather | solution.py:151
  169.6 23.8 %fusion.31 = f32[2,512,1792]{2,1,0:T(8,128)} fusion(bf16[2,512,4096]{2,1,0:T(8,128)(2,1)} %all-gather.2.cloned.1.call-done, bf16[2,4096,1792]{2,1,0:T(8,128)(2,1)} %param.23), kind=kOutput, calls=%fused_computation.95 | convolution fusion | flops 15032385536 | bytes 45088768 | tf_op jit(solution)/shard_map/end,edf->enf/dot_general | solution.py:152
  193.4 24.4 %multiply_convert_fusion = bf16[2,512,1792]{2,1,0:T(8,128)(2,1)} fusion(f32[2,512,1792]{2,1,0:T(8,128)} %fusion.31, bf16[2,512,4096]{2,1,0:T(8,128)(2,1)} %all-gather.2.cloned.1.call-done, bf16[2,4096,1792]{2,1,0:T(8,128)(2,1)} %param.24), kind=kOutput, calls=%fused_computation.5 | convolution fusion | flops 15043395584 | bytes 48758784 | tf_op jit(solution)/shard_map/end,edf->enf/dot_general | solution.py:153
  217.7 23.7 %convert_bitcast_fusion = bf16[512,2,4096]{2,0,1:T(8,128)(2,1)} fusion(bf16[2,512,1792]{2,1,0:T(8,128)(2,1)} %multiply_convert_fusion, bf16[2,1792,4096]{2,1,0:T(8,128)(2,1)} %param.25), kind=kOutput, calls=%fused_computation.4 | convolution fusion | flops 15036579840 | bytes 41418752 | tf_op jit(solution)/shard_map/enf,efd->ned/dot_general | solution.py:156
  242.1 2.0 sort.35
  244.4 4.4 %sort.34 = (s32[1024]{0:T(1024)}, s32[1024]{0:T(1024)S(1)}) sort(s32[1024]{0:T(1024)S(1)} %get-tuple-element.7, s32[1024]{0:T(1024)S(1)} %iota.47), dimensions={0}, to_apply=%region_9.10 | sort | flops 10240 | bytes 16384 | tf_op jit(solution)/shard_map/jit(argsort)/sort | solution.py:71
  248.8 64.3 %reduce-scatter.5.cloned.1.call-done = bf16[64,2,4096]{2,0,1:T(8,128)(2,1)} async-done(((bf16[512,2,4096]{2,0,1:T(8,128)(2,1)}), bf16[64,2,4096]{2,0,1:T(8,128)(2,1)}) %reduce-scatter.5.cloned.1.call-update) | async-done | bytes 1048592 | tf_op jit(solution)/shard_map/reduce_scatter | solution.py:155
  313.1 5.0 %copy.83 = bf16[64,2,4096]{0,1,2:T(2,128)(2,1)S(1)} copy(bf16[64,2,4096]{2,0,1:T(8,128)(2,1)} %reduce-scatter.5.cloned.1.call-done) | data formatting | bytes 2097152 | tf_op jit(solution)/shard_map/reduce_scatter | solution.py:155
  318.1 2.7 reshape.402
  320.9 4.6 %all-to-all-start.1 = ((bf16[4,2,65536]{2,1,0:T(2,128)(2,1)}), bf16[4,2,65536]{2,1,0:T(2,128)(2,1)}, u32[]{:S(2)}, u32[]{:S(2)}) async-start(bf16[4,2,65536]{2,1,0:T(2,128)(2,1)} %reshape.402), calls=%async_computation.3 | async-start | bytes 2097152 | tf_op jit(solution)/shard_map/all_to_all | solution.py:163
  325.5 1.0 gather_fusion.1
  329.4 1.0 pad_maximum_fusion.1
  330.3 21.0 %all-to-all-done.1 = bf16[4,2,65536]{2,1,0:T(2,128)(2,1)} async-done(((bf16[4,2,65536]{2,1,0:T(2,128)(2,1)}), bf16[4,2,65536]{2,1,0:T(2,128)(2,1)}, u32[]{:S(2)}, u32[]{:S(2)}) %all-to-all-start.1) | async-done | bytes 1048608 | tf_op jit(solution)/shard_map/all_to_all | solution.py:163
  351.3 3.1 reshape.403
  354.4 1.8 copy.84
  356.7 1.2 gather_fusion
  358.5 1.3 multiply_reduce_fusion
  (86 shorter events, 11.6 us)
Async XLA Ops:
  7.2 35.8 %copy-start.2 = (bf16[128,1024]{1,0:T(8,128)(2,1)S(1)}, bf16[128,1024]{1,0:T(8,128)(2,1)}, u32[]{:S(2)}) copy-start(bf16[128,1024]{1,0:T(8,128)(2,1)} %param.14) | copy-start | bytes 786436
  7.2 71.0 %reduce-scatter.3.cloned.1.call-start = ((), (), s32[]{:S(2)}) async-start(), calls=%async_computation.4 | async-start | bytes 1310720 | tf_op jit(solution)/shard_map/reduce_scatter | solution.py:116
  44.0 3.1 slice-start
  46.0 2.3 slice-start.1
  48.2 2.4 copy-start.4
  48.2 29.9 %copy-start = (bf16[128,1024]{1,0:T(8,128)(2,1)S(1)}, bf16[128,1024]{1,0:T(8,128)(2,1)}, u32[]{:S(2)}) copy-start(bf16[128,1024]{1,0:T(8,128)(2,1)} %param.13) | copy-start | bytes 786436
  50.5 119.1 %all-gather.2.cloned.1.call-start = ((), (), s32[]{:S(2)}) async-start(), calls=%async_computation.5 | async-start | bytes 9437184 | tf_op jit(solution)/shard_map/all_gather | solution.py:151
  115.9 197.2 %reduce-scatter.5.cloned.1.call-start = ((), (), s32[]{:S(2)}) async-start(), calls=%async_computation.6 | async-start | bytes 9437184 | tf_op jit(solution)/shard_map/reduce_scatter | solution.py:155
  241.5 0.7 copy-start.6
  318.1 10.0 %copy-start.5 = (f32[128,2]{0,1:T(2,128)S(1)}, f32[128,2]{0,1:T(2,128)}, u32[]{:S(2)}) copy-start(f32[128,2]{0,1:T(2,128)} %param.21) | copy-start | bytes 3076
  320.9 30.4 %all-to-all-start.1 = ((bf16[4,2,65536]{2,1,0:T(2,128)(2,1)}), bf16[4,2,65536]{2,1,0:T(2,128)(2,1)}, u32[]{:S(2)}, u32[]{:S(2)}) async-start(bf16[4,2,65536]{2,1,0:T(2,128)(2,1)} %reshape.402), calls=%async_computation.3 | async-start | bytes 2097152 | tf_op jit(solution)/shard_map/all_to_all | solution.py:163
  356.2 2.3 copy-start.3
  356.7 3.2 copy-start.1
Sparse Core Ops, SparseCore 0:
  50.6 27.4 reduce-scatter.2
  116.0 53.5 all-gather.1
  241.6 71.4 reduce-scatter.4
where the time goes:
time: 368 us; the launch traced here: 367 us
  waiting for transfers between devices  166 us (45%)
  matrix products  77.8 us (21%)
  blocking collectives  49.4 us (13%)
  local copies, waits for them, and re-layouts  30 us (8%)
  other arithmetic  25.4 us (7%)
  between operations  14.2 us (4%)
  starting transfers between devices  4.71 us (1%)
    reduce_scatter x1, waiting for transfers between devices, per_device(): lax.psum_scatter(jnp.einsum('enf,efd->ned', hidden_units, w_down, preferr...  64.3 us
    all_gather x1, waiting for transfers between devices, per_device(): token_rows = lax.all_gather(normed, 'seq', axis=1, tiled=True)  53.6 us
    all_to_all x1, blocking collectives, per_device(): lax.all_to_all(outgoing_rows.reshape(exp_count, expert_local * capacity,...  28.2 us
    reduce_scatter x1, waiting for transfers between devices, per_device(): lax.psum_scatter(partial_proj.astype(jnp.bfloat16), 'exp', scatter_dimens...  26.8 us
    dot_general x1, matrix products, per_device(): jnp.einsum('end,edf->enf', token_rows, w_up, preferred_element_type=jnp.f...  24.4 us
    dot_general x1, matrix products, per_device(): jnp.einsum('end,edf->enf', token_rows, w_gate, preferred_element_type=jnp...  23.8 us
    dot_general x1, matrix products, per_device(): jnp.einsum('enf,efd->ned', hidden_units, w_down, preferred_element_type=j...  23.7 us
    all_to_all x1, waiting for transfers between devices, per_device(): lax.all_to_all(returned, 'exp', split_axis=2, concat_axis=1, tiled=True)  21 us
  transfers between devices with their start and end apart: 4, of which 4 were waited for; matrix products, arithmetic and copies ran while one was open for 3% of the time, Pallas kernels for 0%

commit v1 on v0

v1 whole, which is shorter than its diff:
```python
import math

import jax
import jax.numpy as jnp
from jax import lax
from jax.sharding import PartitionSpec as P

HEAD_SIZE = 128
NEXP = 8
PAGE_TOKENS = 16


THETA = 1000000.0
EPS = 1e-05


def apply_rotary(values_in, positions, head_count):
    row_count = values_in.shape[0]
    split_view = values_in.astype(jnp.float32).reshape(row_count, head_count, HEAD_SIZE)
    steps_half = jnp.arange(HEAD_SIZE // 2, dtype=jnp.float32)
    frequency = THETA ** (-(2.0 * steps_half) / HEAD_SIZE)
    angles = positions.astype(jnp.float32)[:, None] * frequency[None, :]
    cosine = jnp.cos(angles)[:, None, :]
    sine_part = jnp.sin(angles)[:, None, :]
    front_half = split_view[..., : HEAD_SIZE // 2]
    back_half = split_view[..., HEAD_SIZE // 2 :]
    turned = jnp.concatenate(
        [front_half * cosine - back_half * sine_part, back_half * cosine + front_half * sine_part],
        axis=-1,
    )
    return turned.reshape(row_count, head_count * HEAD_SIZE).astype(jnp.bfloat16)


def per_device(
    hidden,
    queries,
    keys,
    values,
    block_place,
    page_table,
    out_weight,
    norm_gain,
    gate_probs,
    routes,
    w_gate,
    w_up,
    w_down,
):
    seq_count = lax.axis_size("seq")
    exp_count = lax.axis_size("exp")
    seq_index = lax.axis_index("seq")
    exp_index = lax.axis_index("exp")
    tok_rows = queries.shape[0]
    half_rows = tok_rows // 2
    all_rows = tok_rows * seq_count
    long_len = 3 * all_rows // 4
    blocks = block_place.shape[0]
    within = jnp.arange(half_rows, dtype=jnp.int32)
    all_pos = (block_place[:, None] * half_rows + within[None, :]).reshape(all_rows)
    my_blocks = lax.dynamic_slice_in_dim(block_place, seq_index * 2, 2)
    my_pos = (my_blocks[:, None] * half_rows + within[None, :]).reshape(tok_rows)
    my_long = my_pos >= long_len
    my_rope = my_pos - long_len * my_long.astype(jnp.int32)
    q_heads = queries.shape[1] // HEAD_SIZE
    kv_heads = keys.shape[1] // HEAD_SIZE
    kv_width = keys.shape[1]
    group = q_heads // kv_heads
    key_rotated = apply_rotary(keys, my_rope, kv_heads)
    kv_all = lax.all_gather(
        jnp.concatenate([key_rotated, values], axis=1), "seq", axis=0, tiled=True
    )
    query_rotated = apply_rotary(queries, my_rope, q_heads)
    q_grid = query_rotated.reshape(tok_rows, kv_heads, group, HEAD_SIZE)
    key_all = kv_all[:, :kv_width].reshape(all_rows, kv_heads, HEAD_SIZE)
    value_all = kv_all[:, kv_width:].reshape(all_rows, kv_heads, HEAD_SIZE)
    scores = jnp.einsum(
        "tkgd,nkd->kgtn", q_grid, key_all, preferred_element_type=jnp.float32
    ) * (1.0 / math.sqrt(HEAD_SIZE))
    allowed = ((all_pos >= long_len)[None, :] == my_long[:, None]) & (
        all_pos[None, :] <= my_pos[:, None]
    )
    scores = jnp.where(allowed, scores, -1e30)
    peak = jnp.max(scores, axis=-1)
    weights = jnp.where(allowed, jnp.exp(scores - peak[..., None]), 0.0)
    total = jnp.sum(weights, axis=-1)
    summed = jnp.einsum(
        "kgtn,nkd->kgtd",
        weights.astype(jnp.bfloat16),
        value_all,
        preferred_element_type=jnp.float32,
    )
    attended = (
        (summed / total[..., None])
        .transpose(2, 0, 1, 3)
        .reshape(tok_rows, q_heads * HEAD_SIZE)
        .astype(jnp.bfloat16)
    )
    partial_proj = jnp.dot(attended, out_weight, preferred_element_type=jnp.float32)
    projected = lax.psum_scatter(
        partial_proj.astype(jnp.bfloat16), "exp", scatter_dimension=1, tiled=True
    ).astype(jnp.float32)
    residual = (hidden.astype(jnp.float32) + projected).astype(jnp.bfloat16)

    page_count = tok_rows // PAGE_TOKENS
    page_total = page_table.shape[0]
    per_block = half_rows // PAGE_TOKENS
    my_pages = seq_index * page_count + jnp.arange(page_count, dtype=jnp.int32)
    logical = jnp.sum(
        jnp.where(
            page_table[None, :] == my_pages[:, None],
            jnp.arange(page_total, dtype=jnp.int32)[None, :],
            0,
        ),
        axis=1,
    )
    holder = jnp.sum(
        jnp.where(
            block_place[None, :] == (logical // per_block)[:, None],
            jnp.arange(blocks, dtype=jnp.int32)[None, :],
            0,
        ),
        axis=1,
    )
    source_page = holder * per_block + logical % per_block
    kv_pages = kv_all.reshape(page_total, PAGE_TOKENS, 2 * kv_width)
    cache_pages = jnp.concatenate(
        [lax.dynamic_slice_in_dim(kv_pages, source_page[i], 1) for i in range(page_count)]
    ).reshape(page_count, PAGE_TOKENS, 2, kv_width)

    expert_local = NEXP // exp_count
    capacity = tok_rows // 2
    my_experts = exp_index * expert_local + jnp.arange(expert_local, dtype=jnp.int32)
    hot = routes[:, None, :] == my_experts[None, :, None]
    hit = jnp.any(hot, axis=-1)
    earlier = (jnp.arange(tok_rows)[:, None] > jnp.arange(tok_rows)[None, :]).astype(jnp.bfloat16)
    rank = jnp.dot(
        earlier, hit.astype(jnp.bfloat16), preferred_element_type=jnp.float32
    ).astype(jnp.int32)
    slot_of = jnp.where(hit, rank, -1).T
    chooser = (
        slot_of[:, None, :] == jnp.arange(capacity, dtype=jnp.int32)[None, :, None]
    ).astype(jnp.bfloat16)
    gate_share = gate_probs / jnp.sum(gate_probs, axis=1, keepdims=True)
    share = jnp.sum(jnp.where(hot, gate_share[:, None, :], 0.0), axis=-1)

    residual_full = lax.all_gather(residual, "exp", axis=1, tiled=True).astype(jnp.float32)
    mean_square = jnp.mean(residual_full * residual_full, axis=-1, keepdims=True)
    normed = (residual_full * lax.rsqrt(mean_square + EPS) * norm_gain).astype(jnp.bfloat16)
    token_rows = [
        lax.all_gather(
            jnp.dot(chooser[j], normed, preferred_element_type=jnp.float32).astype(jnp.bfloat16),
            "seq",
            axis=0,
            tiled=True,
        )
        for j in range(expert_local)
    ]
    mixed = 0.0
    for j in range(expert_local):
        gate_part = jnp.dot(token_rows[j], w_gate[j], preferred_element_type=jnp.float32)
        up_part = jnp.dot(token_rows[j], w_up[j], preferred_element_type=jnp.float32)
        units = (jax.nn.silu(gate_part) * up_part).astype(jnp.bfloat16)
        returned = lax.psum_scatter(
            jnp.dot(units, w_down[j], preferred_element_type=jnp.float32).astype(jnp.bfloat16),
            "seq",
            scatter_dimension=0,
            tiled=True,
        )
        placed = lax.dot_general(
            chooser[j], returned, (((0,), (0,)), ((), ())), preferred_element_type=jnp.float32
        )
        mixed = mixed + share[:, j : j + 1] * placed
    chosen = lax.psum_scatter(mixed.astype(jnp.bfloat16), "exp", scatter_dimension=1, tiled=True)
    layer_out = (residual.astype(jnp.float32) + chosen.astype(jnp.float32)).astype(jnp.bfloat16)
    return (layer_out, cache_pages)


def solution(mesh):
    return jax.shard_map(
        per_device,
        mesh=mesh,
        in_specs=(
            P("seq", "exp"),
            P("seq", "exp"),
            P("seq", "exp"),
            P("seq", "exp"),
            P(),
            P(),
            P("exp", None),
            P(),
            P("seq", None),
            P("seq", None),
            P("exp", None, "seq"),
            P("exp", None, "seq"),
            P("exp", "seq", None),
        ),
        out_specs=(P("seq", "exp"), P("seq", None, None, "exp")),
        check_vma=False,
    )
```

time: 368 us -> 343 us (0.932)
  blocking collectives: 49.4 us -> 0 us
  matrix products: 77.8 us -> 125 us
  local copies, waits for them, and re-layouts: 30 us -> 6.39 us
  other arithmetic: 25.4 us -> 9.75 us
  between operations: 14.2 us -> 29.5 us
  waiting for transfers between devices: 166 us -> 170 us
  starting transfers between devices: 4.71 us -> 0.73 us
    dot_general x7 -> x10, matrix products: 75.5 us -> 118 us  [the longest x2 78.6 us: per_device(): jnp.dot(units, w_down[j], preferred_element_type=jnp.float32)]
    all_gather x1 -> x4, waiting for transfers between devices: 53.6 us -> 83.6 us  [the longest x2 33.5 us: per_device(): lax.all_gather(jnp.dot(chooser[j], normed, preferred_element_type=jnp.flo...]
    all_to_all x1 -> x0, blocking collectives: 28.2 us -> none  [per_device(): lax.all_to_all(outgoing_rows.reshape(exp_count, expert_local * capacity,...]
    all_gather x2 -> x0, blocking collectives: 21.2 us -> none  [the longest x1 11.3 us: per_device(): lax.all_gather(key_rotated, 'seq', axis=0, tiled=True)]
    all_to_all x1 -> x0, waiting for transfers between devices: 21 us -> none  [per_device(): lax.all_to_all(returned, 'exp', split_axis=2, concat_axis=1, tiled=True)]
    sort x2 -> x0, other arithmetic: 6.4 us -> none  [the longest x1 4.37 us: per_device(): row_at = jnp.argsort(all_pos)]
    convert_element_type x5 -> x0, local copies, waits for them, and re-layouts: 6.25 us -> none  [the longest x2 5.4 us: per_device(): arrived_rows.reshape(expert_local, capacity, -1).astype(jnp.float32)]
    unnamed x23 -> x25, local copies, waits for them, and re-layouts: 7.75 us -> 1.73 us
  transfers between devices with their start and end apart: 4 -> 8, of which waited for: 4 -> 6; matrix products, arithmetic and copies ran while one was open for 3% -> 34% of each run, Pallas kernels for 0% -> 0%
where the time goes in v1:
time: 343 us; the launch traced here: 342 us
  waiting for transfers between devices  170 us (50%)
  matrix products  125 us (36%)
  between operations  29.5 us (9%)
  other arithmetic  9.75 us (3%)
  local copies, waits for them, and re-layouts  6.39 us (2%)
    dot_general x2, matrix products, per_device(): jnp.dot(units, w_down[j], preferred_element_type=jnp.float32)  78.6 us
    reduce_scatter x2, waiting for transfers between devices, per_device(): lax.psum_scatter(jnp.dot(units, w_down[j], preferred_element_type=jnp.flo...  49.5 us
    all_gather x2, waiting for transfers between devices, per_device(): lax.all_gather(jnp.dot(chooser[j], normed, preferred_element_type=jnp.flo...  33.5 us
    dot_general x2, matrix products, per_device(): jnp.dot(token_rows[j], w_gate[j], preferred_element_type=jnp.float32)  29.3 us
    reduce_scatter x1, waiting for transfers between devices, per_device(): lax.psum_scatter(partial_proj.astype(jnp.bfloat16), 'exp', scatter_dimens...  27.2 us
    all_gather x1, waiting for transfers between devices, per_device(): lax.all_gather(residual, 'exp', axis=1, tiled=True).astype(jnp.float32)  26.8 us
    all_gather x1, waiting for transfers between devices, per_device(): lax.all_gather(jnp.concatenate([key_rotated, values], axis=1), 'seq', axi...  23.3 us
    reduce_scatter x1, waiting for transfers between devices, per_device(): lax.psum_scatter(mixed.astype(jnp.bfloat16), 'exp', scatter_dimension=1,...  9.79 us
  transfers between devices with their start and end apart: 8, of which 6 were waited for; matrix products, arithmetic and copies ran while one was open for 34% of the time, Pallas kernels for 0%

profile of v1, /device:TPU:0, one launch (start us, length us, event | category | flops | bytes accessed | tf_op | source)
XLA Modules:
  0.0 342.0 jit_solution(9220760642314263024)
XLA Ops:
  7.2 0.7 dynamic-slice_multiply_fusion
  8.1 0.9 copy.70
  9.1 1.0 copy.57
  10.3 0.7 pad_maximum_fusion.1
  11.0 1.0 convert_bitcast_fusion
  12.3 0.7 broadcast_multiply_fusion
  13.7 0.3 compare_and_fusion
  14.1 23.3 %all-gather.5.cloned.1.call-done = bf16[1024,512]{0,1:T(8,128)(2,1)} async-done(((bf16[128,512]{0,1:T(8,128)(2,1)}), bf16[1024,512]{0,1:T(8,128)(2,1)}) %all-gather.5.cloned.1.call-update) | async-done | bytes 1048592 | tf_op jit(solution)/shard_map/all_gather | solution.py:69
  37.4 1.3 fusion.66
  38.7 2.0 fusion.69
  40.7 0.5 fusion.52
  41.2 5.7 %convolution_convert_fusion = bf16[128,4096]{1,0:T(8,128)(2,1)} fusion(bf16[128,1024]{0,1:T(8,128)(2,1)S(1)} %bitcast.112, bf16[1024,4096]{1,0:T(8,128)(2,1)} %param.19), kind=kOutput, calls=%fused_computation.25 | convolution fusion | flops 1074266112 | bytes 9699328 | tf_op jit(solution)/shard_map/dot_general | solution.py:98
  47.0 27.2 %reduce-scatter.5.cloned.1.call-done = bf16[128,1024]{1,0:T(8,128)(2,1)} async-done(((bf16[128,4096]{1,0:T(8,128)(2,1)}), bf16[128,1024]{1,0:T(8,128)(2,1)}) %reduce-scatter.5.cloned.1.call-update) | async-done | bytes 262160 | tf_op jit(solution)/shard_map/reduce_scatter | solution.py:99
  74.3 1.7 add_convert_fusion.1
  76.3 26.8 %all-gather.7.cloned.1.call-done = bf16[128,4096]{1,0:T(8,128)(2,1)} async-done(((bf16[128,1024]{1,0:T(8,128)(2,1)}), bf16[128,4096]{1,0:T(8,128)(2,1)}) %all-gather.7.cloned.1.call-update) | async-done | bytes 1048592 | tf_op jit(solution)/shard_map/all_gather | solution.py:146
  103.1 1.5 fusion.36
  104.6 2.5 convolution_convert_fusion.2
  107.2 2.5 convolution_convert_fusion.1
  110.0 33.5 %all-gather.9.cloned.1.call-done = bf16[512,4096]{1,0:T(8,128)(2,1)} async-done(((bf16[64,4096]{1,0:T(8,128)(2,1)}), bf16[512,4096]{1,0:T(8,128)(2,1)}) %all-gather.9.cloned.1.call-update) | async-done | bytes 4194320 | tf_op jit(solution)/shard_map/all_gather | solution.py:150
  143.5 14.6 %fusion.11 = f32[512,1792]{1,0:T(8,128)} fusion(bf16[512,4096]{1,0:T(8,128)(2,1)} %all-gather.9.cloned.1.call-done, bf16[2,4096,1792]{2,1,0:T(8,128)(2,1)} %param.23), kind=kOutput, calls=%fused_computation.11 | convolution fusion | flops 7516192768 | bytes 22544384 | tf_op jit(solution)/shard_map/dot_general | solution.py:160
  158.1 39.3 %fusion.19 = bf16[512,4096]{1,0:T(8,128)(2,1)} fusion(bf16[2,1792,4096]{2,1,0:T(8,128)(2,1)} %param.25, f32[512,1792]{1,0:T(8,128)} %fusion.11, bf16[512,4096]{1,0:T(8,128)(2,1)} %all-gather.9.cloned.1.call-done, bf16[2,4096,1792]{2,1,0:T(8,128)(2,1)} %param.24), kind=kOutput, calls=%fused_computation.19 | convolution fusion | flops 15039987712 | bytes 41418752 | tf_op jit(solution)/shard_map/dot_general | solution.py:164
  197.7 14.7 %fusion.5 = f32[512,1792]{1,0:T(8,128)} fusion(bf16[512,4096]{1,0:T(8,128)(2,1)} %all-gather.11.cloned.1.call-done, bf16[2,4096,1792]{2,1,0:T(8,128)(2,1)} %param.23), kind=kOutput, calls=%fused_computation.5 | convolution fusion | flops 7516192768 | bytes 22544384 | tf_op jit(solution)/shard_map/dot_general | solution.py:160
  212.4 39.3 %fusion.22 = bf16[512,4096]{1,0:T(8,128)(2,1)} fusion(bf16[2,1792,4096]{2,1,0:T(8,128)(2,1)} %param.25, f32[512,1792]{1,0:T(8,128)} %fusion.5, bf16[512,4096]{1,0:T(8,128)(2,1)} %all-gather.11.cloned.1.call-done, bf16[2,4096,1792]{2,1,0:T(8,128)(2,1)} %param.24), kind=kOutput, calls=%fused_computation.20 | convolution fusion | flops 15039987712 | bytes 41418752 | tf_op jit(solution)/shard_map/dot_general | solution.py:164
  251.8 0.6 copy-done.4
  252.5 1.5 convolution_multiply_fusion.1
  254.1 49.5 %reduce-scatter.9.cloned.1.call-done = bf16[64,4096]{1,0:T(8,128)(2,1)} async-done(((bf16[512,4096]{1,0:T(8,128)(2,1)}), bf16[64,4096]{1,0:T(8,128)(2,1)}) %reduce-scatter.9.cloned.1.call-update) | async-done | bytes 524304 | tf_op jit(solution)/shard_map/reduce_scatter | solution.py:163
  303.6 2.5 fusion.26
  306.5 0.7 fusion.68
  322.2 0.5 copy.64
  322.9 0.7 reshape.200
  323.6 9.8 %reduce-scatter.11.cloned.1.call-done = bf16[128,1024]{1,0:T(8,128)(2,1)} async-done(((bf16[128,4096]{1,0:T(8,128)(2,1)}), bf16[128,1024]{1,0:T(8,128)(2,1)}) %reduce-scatter.11.cloned.1.call-update) | async-done | bytes 262160 | tf_op jit(solution)/shard_map/reduce_scatter | solution.py:173
  333.4 1.7 add_convert_fusion
  (72 shorter events, 3.2 us)
Async XLA Ops:
  7.2 30.2 %all-gather.5.cloned.1.call-start = ((), (), s32[]{:S(2)}) async-start(), calls=%async_computation.4 | async-start | bytes 1179648 | tf_op jit(solution)/shard_map/all_gather | solution.py:69
  11.0 63.3 %reduce-scatter.5.cloned.1.call-start = ((), (), s32[]{:S(2)}) async-start(), calls=%async_computation.5 | async-start | bytes 1310720 | tf_op jit(solution)/shard_map/reduce_scatter | solution.py:99
  41.2 33.0 %copy-start.2 = (bf16[128,1024]{1,0:T(8,128)(2,1)S(1)}, bf16[128,1024]{1,0:T(8,128)(2,1)}, u32[]{:S(2)}) copy-start(bf16[128,1024]{1,0:T(8,128)(2,1)} %param.13) | copy-start | bytes 786436
  41.2 34.8 %copy-start.3 = (s32[128,2]{0,1:T(2,128)S(1)}, s32[128,2]{0,1:T(2,128)}, u32[]{:S(2)}) copy-start(s32[128,2]{0,1:T(2,128)} %param.22) | copy-start | bytes 3076
  41.2 63.4 %copy-start.5 = (f32[4096]{0:T(1024)S(1)}, f32[4096]{0:T(1024)}, u32[]{:S(2)}) copy-start(f32[4096]{0:T(1024)} %param.20) | copy-start | bytes 49156
  47.0 56.1 %all-gather.7.cloned.1.call-start = ((), (), s32[]{:S(2)}) async-start(), calls=%async_computation.6 | async-start | bytes 1310720 | tf_op jit(solution)/shard_map/all_gather | solution.py:146
  76.0 67.5 %all-gather.9.cloned.1.call-start = ((), (), s32[]{:S(2)}) async-start(), calls=%async_computation.7 | async-start | bytes 4718592 | tf_op jit(solution)/shard_map/all_gather | solution.py:150
  107.2 90.5 %all-gather.11.cloned.1.call-start = ((), (), s32[]{:S(2)}) async-start(), calls=%async_computation.9 | async-start | bytes 4718592 | tf_op jit(solution)/shard_map/all_gather | solution.py:150
  109.8 142.8 %reduce-scatter.7.cloned.1.call-start = ((), (), s32[]{:S(2)}) async-start(), calls=%async_computation.8 | async-start | bytes 4718592 | tf_op jit(solution)/shard_map/reduce_scatter | solution.py:163
  197.4 106.2 %reduce-scatter.9.cloned.1.call-start = ((), (), s32[]{:S(2)}) async-start(), calls=%async_computation.10 | async-start | bytes 4718592 | tf_op jit(solution)/shard_map/reduce_scatter | solution.py:163
  251.7 0.7 copy-start.4
  251.7 54.4 %copy-start.6 = (s32[64]{0:T(128)S(1)}, s32[64]{0:T(128)}, u32[]{:S(2)}) copy-start(s32[64]{0:T(128)} %param.18) | copy-start | bytes 772
  251.7 54.6 %copy-start.7 = (s32[16]{0:T(128)S(1)}, s32[16]{0:T(128)}, u32[]{:S(2)}) copy-start(s32[16]{0:T(128)} %param.17) | copy-start | bytes 196
  251.8 70.5 %copy-start = (bf16[1024,512]{0,1:T(8,128)(2,1)S(1)}, bf16[1024,512]{0,1:T(8,128)(2,1)}, u32[]{:S(2)}) copy-start(bf16[1024,512]{0,1:T(8,128)(2,1)} %all-gather.5.cloned.1.call-done) | copy-start | bytes 3145732
  251.8 81.6 %reduce-scatter.11.cloned.1.call-start = ((), (), s32[]{:S(2)}) async-start(), calls=%async_computation.11 | async-start | bytes 1310720 | tf_op jit(solution)/shard_map/reduce_scatter | solution.py:173
  254.1 79.3 %copy-start.1 = (bf16[128,1024]{1,0:T(8,128)(2,1)S(1)}, bf16[128,1024]{1,0:T(8,128)(2,1)}, u32[]{:S(2)}) copy-start(bf16[128,1024]{1,0:T(8,128)(2,1)} %add_convert_fusion.1) | copy-start | bytes 786436
Sparse Core Ops, SparseCore 0:
  11.1 26.2 all-gather.4
  47.1 27.1 reduce-scatter.4
  76.5 26.5 all-gather.6
  107.3 36.1 all-gather.8
  145.4 36.7 all-gather.10
  197.5 51.3 reduce-scatter.6
  252.2 51.3 reduce-scatter.8
  306.2 27.1 reduce-scatter.10

commit v2 on v1

--- a/solution.py
+++ b/solution.py
@@ -1,8 +1,11 @@
+import functools
 import math
 
 import jax
 import jax.numpy as jnp
 from jax import lax
+from jax.experimental import pallas as pl
+from jax.experimental.pallas import tpu as pltpu
 from jax.sharding import PartitionSpec as P
 
 HEAD_SIZE = 128
@@ -29,6 +32,179 @@
         axis=-1,
     )
     return turned.reshape(row_count, head_count * HEAD_SIZE).astype(jnp.bfloat16)
+
+
+MESH = pl.DeviceIdType.MESH
+
+
+def divisor_tile(size, choices):
+    for choice in choices:
+        if size % choice == 0:
+            return choice
+    return size
+
+
+def experts_kernel(
+    n, x_ref, wg_ref, wu_ref, wd_ref, out_ref,
+    rows, units, part, inbox, gs, gr, rs, rr,
+):
+    experts, cap, width = x_ref.shape
+    inner = wg_ref.shape[2]
+    total_rows = n * cap
+    step_rows = 256
+    me = lax.axis_index("seq")
+    exp_me = lax.axis_index("exp")
+
+    def peer(k):
+        return (lax.rem(me + k, n), exp_me)
+
+    def rows_of(index):
+        return pl.ds(pl.multiple_of(index * cap, cap), cap)
+
+    barrier = pltpu.get_barrier_semaphore()
+    for k in range(1, n):
+        pl.semaphore_signal(barrier, inc=1, device_id=peer(k), device_id_type=MESH)
+    pl.semaphore_wait(barrier, n - 1)
+
+    def gather_copy(e, k):
+        return pltpu.make_async_remote_copy(
+            src_ref=x_ref.at[e],
+            dst_ref=rows.at[e, rows_of(me)],
+            send_sem=gs.at[e, k - 1],
+            recv_sem=gr.at[e, k - 1],
+            device_id=peer(k),
+            device_id_type=MESH,
+        )
+
+    def return_copy(e, h, k):
+        half = width // 2
+        columns = pl.ds(h * half, half)
+        return pltpu.make_async_remote_copy(
+            src_ref=part.at[e, rows_of(lax.rem(me + k, n)), columns],
+            dst_ref=inbox.at[e, rows_of(me), columns],
+            send_sem=rs.at[e, h, k - 1],
+            recv_sem=rr.at[e, h, k - 1],
+            device_id=peer(k),
+            device_id_type=MESH,
+        )
+
+    gate_tile = divisor_tile(inner, (256, 128))
+    down_tile = 512
+
+    def start_gather(e):
+        for k in range(1, n):
+            gather_copy(e, k).start()
+        rows[e, rows_of(me)] = x_ref[e]
+
+    def end_gather(e):
+        for k in range(1, n):
+            gather_copy(e, k).wait_recv()
+
+    start_gather(0)
+    for e in range(experts):
+        end_gather(e)
+        if e + 1 < experts:
+            start_gather(e + 1)
+
+        def gate_body(wg_tile, wu_tile, e=e):
+            column = pl.multiple_of(pl.program_id(0) * gate_tile, gate_tile)
+
+            @pl.loop(0, total_rows // step_rows)
+            def _(m):
+                at = pl.ds(pl.multiple_of(m * step_rows, step_rows), step_rows)
+                x = rows[e, at]
+                gate = jnp.dot(x, wg_tile[...], preferred_element_type=jnp.float32)
+                up = jnp.dot(x, wu_tile[...], preferred_element_type=jnp.float32)
+                units[at, pl.ds(column, gate_tile)] = (
+                    gate / (1.0 + jnp.exp(-gate)) * up
+                ).astype(jnp.bfloat16)
+
+        spec = pl.BlockSpec((width, gate_tile), lambda j: (0, j))
+        pltpu.emit_pipeline(
+            gate_body,
+            grid=(inner // gate_tile,),
+            in_specs=[spec, spec],
+            out_specs=[],
+        )(wg_ref.at[e], wu_ref.at[e])
+
+        for h in range(2):
+
+            def down_body(wd_tile, e=e, h=h):
+                column = pl.multiple_of(h * (width // 2) + pl.program_id(0) * down_tile, down_tile)
+
+                @pl.loop(0, total_rows // step_rows)
+                def _(m):
+                    at = pl.ds(pl.multiple_of(m * step_rows, step_rows), step_rows)
+                    part[e, at, pl.ds(column, down_tile)] = jnp.dot(
+                        units[at], wd_tile[...], preferred_element_type=jnp.float32
+                    ).astype(jnp.bfloat16)
+
+            per_half = width // 2 // down_tile
+            pltpu.emit_pipeline(
+                down_body,
+                grid=(per_half,),
+                in_specs=[
+                    pl.BlockSpec((inner, down_tile), lambda j, h=h: (0, h * per_half + j))
+                ],
+                out_specs=[],
+            )(wd_ref.at[e])
+            for k in range(1, n):
+                return_copy(e, h, k).start()
+
+    for e in range(experts):
+        for h in range(2):
+            for k in range(1, n):
+                return_copy(e, h, k).wait_recv()
+        piece = 16
+
+        @pl.loop(0, cap // piece)
+        def _(r):
+            at = pl.multiple_of(r * piece, piece)
+            total = part[e, pl.ds(pl.multiple_of(me * cap + at, piece), piece)].astype(jnp.float32)
+            for k in range(1, n):
+                sender = lax.rem(me + n - k, n)
+                total += inbox[
+                    e, pl.ds(pl.multiple_of(sender * cap + at, piece), piece)
+                ].astype(jnp.float32)
+            out_ref[e, pl.ds(at, piece)] = total.astype(jnp.bfloat16)
+
+    for e in range(experts):
+        for k in range(1, n):
+            gather_copy(e, k).wait_send()
+            for h in range(2):
+                return_copy(e, h, k).wait_send()
+
+
+def run_experts(n, x, w_gate, w_up, w_down):
+    experts, cap, width = x.shape
+    inner = w_gate.shape[2]
+    vmem = pl.BlockSpec(memory_space=pltpu.VMEM)
+    anywhere = pl.BlockSpec(memory_space=pl.ANY)
+    big = pltpu.VMEM((experts, n * cap, width), jnp.bfloat16)
+    return pl.pallas_call(
+        functools.partial(experts_kernel, n),
+        out_shape=jax.ShapeDtypeStruct(x.shape, jnp.bfloat16),
+        in_specs=[vmem, anywhere, anywhere, anywhere],
+        out_specs=vmem,
+        scratch_shapes=[
+            big,
+            pltpu.VMEM((n * cap, inner), jnp.bfloat16),
+            big,
+            big,
+            pltpu.SemaphoreType.DMA((experts, n - 1)),
+            pltpu.SemaphoreType.DMA((experts, n - 1)),
+            pltpu.SemaphoreType.DMA((experts, 2, n - 1)),
+            pltpu.SemaphoreType.DMA((experts, 2, n - 1)),
+        ],
+        compiler_params=pltpu.CompilerParams(
+            collective_id=0, has_side_effects=True, vmem_limit_bytes=56 * 1024 * 1024
+        ),
+        cost_estimate=pl.CostEstimate(
+            flops=6 * experts * n * cap * width * inner,
+            bytes_accessed=6 * experts * width * inner,
+            transcendentals=experts * n * cap * inner,
+        ),
+    )(x, w_gate, w_up, w_down)
 
 
 def per_device(
@@ -146,28 +322,14 @@
     residual_full = lax.all_gather(residual, "exp", axis=1, tiled=True).astype(jnp.float32)
     mean_square = jnp.mean(residual_full * residual_full, axis=-1, keepdims=True)
     normed = (residual_full * lax.rsqrt(mean_square + EPS) * norm_gain).astype(jnp.bfloat16)
-    token_rows = [
-        lax.all_gather(
-            jnp.dot(chooser[j], normed, preferred_element_type=jnp.float32).astype(jnp.bfloat16),
-            "seq",
-            axis=0,
-            tiled=True,
-        )
-        for j in range(expert_local)
-    ]
+    slots = jnp.einsum(
+        "est,td->esd", chooser, normed, preferred_element_type=jnp.float32
+    ).astype(jnp.bfloat16)
+    returned = run_experts(seq_count, slots, w_gate, w_up, w_down)
     mixed = 0.0
     for j in range(expert_local):
-        gate_part = jnp.dot(token_rows[j], w_gate[j], preferred_element_type=jnp.float32)
-        up_part = jnp.dot(token_rows[j], w_up[j], preferred_element_type=jnp.float32)
-        units = (jax.nn.silu(gate_part) * up_part).astype(jnp.bfloat16)
-        returned = lax.psum_scatter(
-            jnp.dot(units, w_down[j], preferred_element_type=jnp.float32).astype(jnp.bfloat16),
-            "seq",
-            scatter_dimension=0,
-            tiled=True,
-        )
         placed = lax.dot_general(
-            chooser[j], returned, (((0,), (0,)), ((), ())), preferred_element_type=jnp.float32
+            chooser[j], returned[j], (((0,), (0,)), ((), ())), preferred_element_type=jnp.float32
         )
         mixed = mixed + share[:, j : j + 1] * placed
     chosen = lax.psum_scatter(mixed.astype(jnp.bfloat16), "exp", scatter_dimension=1, tiled=True)

time: 343 us -> 334 us (0.974)
  Pallas kernels: 0 us -> 185 us
  matrix products: 125 us -> 14.3 us
  waiting for transfers between devices: 170 us -> 88.1 us
    pallas_call x0 -> x1, Pallas kernels: none -> 185 us  [run_experts(): pl.pallas_call(functools.partial(experts_kernel, n), out_shape=jax.ShapeD...]
    dot_general x8 -> x3, matrix products: 117 us -> 5.91 us  [the longest x2 3.14 us: per_device(): lax.dot_general(chooser[j], returned[j], (((0,), (0,)), ((), ())), prefer...]
    reduce_scatter x2 -> x0, waiting for transfers between devices: 49.5 us -> none  [per_device(): lax.psum_scatter(jnp.dot(units, w_down[j], preferred_element_type=jnp.flo...]
    all_gather x2 -> x0, waiting for transfers between devices: 33.5 us -> none  [per_device(): lax.all_gather(jnp.dot(chooser[j], normed, preferred_element_type=jnp.flo...]
  transfers between devices with their start and end apart: 8 -> 4, of which waited for: 6 -> 4; matrix products, arithmetic and copies ran while one was open for 34% -> 2% of each run, Pallas kernels for 0% -> 0%
where the time goes in v2:
time: 334 us; the launch traced here: 333 us
  Pallas kernels  185 us (55%)
  waiting for transfers between devices  88.1 us (26%)
  between operations  28.9 us (9%)
  matrix products  14.3 us (4%)
  other arithmetic  9.74 us (3%)
  local copies, waits for them, and re-layouts  5.83 us (2%)
    pallas_call x1, Pallas kernels, run_experts(): pl.pallas_call(functools.partial(experts_kernel, n), out_shape=jax.ShapeD...  185 us
    reduce_scatter x1, waiting for transfers between devices, per_device(): lax.psum_scatter(partial_proj.astype(jnp.bfloat16), 'exp', scatter_dimens...  27.2 us
    all_gather x1, waiting for transfers between devices, per_device(): lax.all_gather(residual, 'exp', axis=1, tiled=True).astype(jnp.float32)  26.5 us
    all_gather x1, waiting for transfers between devices, per_device(): lax.all_gather(jnp.concatenate([key_rotated, values], axis=1), 'seq', axi...  23.3 us
    reduce_scatter x1, waiting for transfers between devices, per_device(): lax.psum_scatter(mixed.astype(jnp.bfloat16), 'exp', scatter_dimension=1,...  11 us
  transfers between devices with their start and end apart: 4, of which 4 were waited for; matrix products, arithmetic and copies ran while one was open for 2% of the time, Pallas kernels for 0%

profile of v2, /device:TPU:0, one launch (start us, length us, event | category | flops | bytes accessed | tf_op | source)
XLA Modules:
  0.0 332.7 jit_solution(463337096761671466)
XLA Ops:
  7.2 0.7 dynamic-slice_multiply_fusion
  8.1 0.9 copy.57
  9.1 0.9 copy.70
  10.0 0.2 multiply_cosine_fusion
  10.3 0.7 pad_maximum_fusion.1
  11.0 0.7 broadcast_multiply_fusion
  12.0 1.0 convert_bitcast_fusion
  13.1 0.2 fusion.37
  13.3 0.2 subtract_convert_fusion
  13.5 0.1 pad_maximum_fusion
  13.7 0.3 compare_and_fusion
  14.1 23.3 %all-gather.3.cloned.1.call-done = bf16[1024,512]{0,1:T(8,128)(2,1)} async-done(((bf16[128,512]{0,1:T(8,128)(2,1)}), bf16[1024,512]{0,1:T(8,128)(2,1)}) %all-gather.3.cloned.1.call-update) | async-done | bytes 1048592 | tf_op jit(solution)/shard_map/all_gather | solution.py:245
  37.4 1.3 fusion.36
  38.7 2.0 fusion.39
  40.7 0.5 fusion.18
  41.2 5.8 %convolution_convert_fusion.1 = bf16[128,4096]{1,0:T(8,128)(2,1)} fusion(bf16[128,1024]{0,1:T(8,128)(2,1)S(1)} %bitcast.83, bf16[1024,4096]{1,0:T(8,128)(2,1)} %param.19), kind=kOutput, calls=%fused_computation.6 | convolution fusion | flops 1074266112 | bytes 9699328 | tf_op jit(solution)/shard_map/dot_general | solution.py:274
  47.1 27.2 %reduce-scatter.3.cloned.1.call-done = bf16[128,1024]{1,0:T(8,128)(2,1)} async-done(((bf16[128,4096]{1,0:T(8,128)(2,1)}), bf16[128,1024]{1,0:T(8,128)(2,1)}) %reduce-scatter.3.cloned.1.call-update) | async-done | bytes 262160 | tf_op jit(solution)/shard_map/reduce_scatter | solution.py:275
  74.3 1.7 add_convert_fusion.1
  76.1 0.2 reduce-scatter.5.cloned.1.call-start
  76.7 26.5 %all-gather.5.cloned.1.call-done = bf16[128,4096]{1,0:T(8,128)(2,1)} async-done(((bf16[128,1024]{1,0:T(8,128)(2,1)}), bf16[128,4096]{1,0:T(8,128)(2,1)}) %all-gather.5.cloned.1.call-update) | async-done | bytes 1048592 | tf_op jit(solution)/shard_map/all_gather | solution.py:322
  103.2 1.5 fusion.4
  104.7 2.8 convolution_convert_fusion.x_ref
  107.5 185.4 %shard_map.140 = bf16[2,64,4096]{2,1,0:T(8,128)(2,1)} custom-call(bf16[2,64,4096]{2,1,0:T(8,128)(2,1)} %convolution_convert_fusion.x_ref, bf16[2,4096,1792]{2,1,0:T(8,128)(2,1)} %wg_ref.1, bf16[2,4096,1792]{2,1,0:T(8,128)(2,1)} %wu_ref.1, bf16[2,1792,4096]{2,1,0:T(8,128)(2,1)} %wd_ref.1), custom_call_target="tpu_custom_call" | custom-call | flops 45097156608 | bytes 88080384 | tf_op jit(solution)/shard_map/pallas_call | solution.py:184
  293.0 1.6 convolution_multiply_fusion.1
  294.6 1.5 fusion.2
  296.2 0.2 select_reduce_fusion.1
  296.4 0.2 select_reduce_fusion
  296.6 0.7 fusion.38
  312.1 0.5 copy.64
  312.8 0.7 reshape.200
  313.5 11.0 %reduce-scatter.5.cloned.1.call-done = bf16[128,1024]{1,0:T(8,128)(2,1)} async-done(((bf16[128,4096]{1,0:T(8,128)(2,1)}), bf16[128,1024]{1,0:T(8,128)(2,1)}) %reduce-scatter.5.cloned.1.call-update) | async-done | bytes 262160 | tf_op jit(solution)/shard_map/reduce_scatter | solution.py:335
  324.5 1.7 add_convert_fusion
  (58 shorter events, 1.4 us)
Async XLA Ops:
  7.2 30.2 %all-gather.3.cloned.1.call-start = ((), (), s32[]{:S(2)}) async-start(), calls=%async_computation.2 | async-start | bytes 1179648 | tf_op jit(solution)/shard_map/all_gather | solution.py:245
  11.0 63.3 %reduce-scatter.3.cloned.1.call-start = ((), (), s32[]{:S(2)}) async-start(), calls=%async_computation.3 | async-start | bytes 1310720 | tf_op jit(solution)/shard_map/reduce_scatter | solution.py:275
  41.2 33.1 %copy-start.3 = (bf16[128,1024]{1,0:T(8,128)(2,1)S(1)}, bf16[128,1024]{1,0:T(8,128)(2,1)}, u32[]{:S(2)}) copy-start(bf16[128,1024]{1,0:T(8,128)(2,1)} %param.13) | copy-start | bytes 786436
  47.0 29.3 %copy-start.6 = (f32[128,2]{0,1:T(2,128)S(1)}, f32[128,2]{0,1:T(2,128)}, u32[]{:S(2)}) copy-start(f32[128,2]{0,1:T(2,128)} %param.21) | copy-start | bytes 3076
  47.0 29.4 %copy-start.5 = (s32[128,2]{0,1:T(2,128)S(1)}, s32[128,2]{0,1:T(2,128)}, u32[]{:S(2)}) copy-start(s32[128,2]{0,1:T(2,128)} %param.22) | copy-start | bytes 3076
  47.0 57.7 %copy-start.4 = (f32[4096]{0:T(1024)S(1)}, f32[4096]{0:T(1024)}, u32[]{:S(2)}) copy-start(f32[4096]{0:T(1024)} %param.20) | copy-start | bytes 49156
  47.0 56.2 %all-gather.5.cloned.1.call-start = ((), (), s32[]{:S(2)}) async-start(), calls=%async_computation.4 | async-start | bytes 1310720 | tf_op jit(solution)/shard_map/all_gather | solution.py:322
  76.1 248.4 %reduce-scatter.5.cloned.1.call-start = ((), (), s32[]{:S(2)}) async-start(), calls=%async_computation.5 | async-start | bytes 1310720 | tf_op jit(solution)/shard_map/reduce_scatter | solution.py:335
  292.9 1.6 copy-start.2
  294.6 1.6 copy-start.7
  294.6 1.8 copy-start.8
  294.6 17.5 %copy-start = (bf16[1024,512]{0,1:T(8,128)(2,1)S(1)}, bf16[1024,512]{0,1:T(8,128)(2,1)}, u32[]{:S(2)}) copy-start(bf16[1024,512]{0,1:T(8,128)(2,1)} %all-gather.3.cloned.1.call-done) | copy-start | bytes 3145732
  296.1 28.3 %copy-start.1 = (bf16[128,1024]{1,0:T(8,128)(2,1)S(1)}, bf16[128,1024]{1,0:T(8,128)(2,1)}, u32[]{:S(2)}) copy-start(bf16[128,1024]{1,0:T(8,128)(2,1)} %add_convert_fusion.1) | copy-start | bytes 786436
Sparse Core Ops, SparseCore 0:
  11.1 26.2 all-gather.2
  47.1 27.1 reduce-scatter.2
  76.5 26.5 all-gather.4
  296.3 28.1 reduce-scatter.4
